TPU v7x, 32 devices: a whole 2x2x4 slice. The times are simulated.
32 devices in a mesh: harm: 2 (over x), space: 16 (over z, y, core).
Axes of the slice: x: 2, y: 2, z: 4, core: 2. Of those that a mesh axis runs over, the one named last changes fastest.
Arguments:
- rhs_field: float32 [64, 4096], P('harm', 'space'), may hold values from -14 to 14
- neighbors: int32 [8, 4096], P(None, 'space'), may hold values from 0 to 4095, as said below
- nu_mean: float32 [8, 4096], P(None, 'space'), may hold values from 0.5 to 4
- nu_ripple: float32 [64, 8, 4096], P(None, None, 'space'), may hold values from -0.24 to 0.24
- mass_coeff: float32 [4096], P('space'), may hold values from 0.5 to 2
- eddy_coeff: float32 [4096], P('space'), may hold values from 0.25 to 2
Outputs:
- correction: float32 [64, 4096], P('harm', 'space')
- residual: float32 [64, 4096], P('harm', 'space')
Inputs may be any that keep to these rules, and one draw needn't show every extreme that they name: neighbors[d, n] is a node at most 64 places from n in the node order closed into a loop (node 4095 lies next to node 0), or n itself for an unused slot; slot 0 is always used, and some entry lies 64 places away in each direction.
All inputs are finite; a program needn't handle non-finite values.
Results may differ from a plain program's by a relative error of at most 0.0003.
Values sent between devices are 32-bit elements; how exact they have to be, the bound alone decides.
A program may use at most 64 MiB of HBM per device.

v0:
```python
import jax
import jax.numpy as jnp
from jax import lax
from jax.sharding import PartitionSpec as P

IF = 64
ITERS = 8


def with_halo(array, sides, width):
    for axis, dim in sides:
        count, length = (lax.axis_size(axis), array.shape[dim])
        up = [(i, (i + 1) % count) for i in range(count)]
        down = [(j, i) for i, j in up]
        last = lax.slice_in_dim(array, length - width, length, axis=dim)
        leading = lax.slice_in_dim(array, 0, width, axis=dim)
        before = lax.ppermute(last, axis, up)
        after = lax.ppermute(leading, axis, down)
        array = jnp.concatenate([before, array, after], axis=dim)
    return array


def swap_pairs(vector_in):
    shaped = vector_in.reshape(vector_in.shape[0] // 2, 2, vector_in.shape[1])
    return shaped[:, ::-1, :].reshape(vector_in.shape)


def fourier_tables(harmonics):
    index_vals = jnp.arange(harmonics, dtype=jnp.int32)
    product_mod = jnp.mod(index_vals[:, None] * index_vals[None, :], harmonics).astype(jnp.float32)
    phase = 2.0 * jnp.pi * product_mod / harmonics
    return (jnp.cos(phase), jnp.sin(phase))


def matmul_high(left, right):
    return jnp.dot(left, right, precision=lax.Precision.HIGHEST, preferred_element_type=jnp.float32)


def least_squares(columns, beta_norm):
    steps_total = len(columns)
    rot_cos, rot_sin = ([], [])
    target = [beta_norm] + [jnp.zeros((), jnp.float32)] * steps_total
    triangle = []
    for j in range(steps_total):
        column_vals = list(columns[j])
        for i in range(j):
            first, second = (column_vals[i], column_vals[i + 1])
            column_vals[i] = rot_cos[i] * first + rot_sin[i] * second
            column_vals[i + 1] = rot_cos[i] * second - rot_sin[i] * first
        radius = jnp.sqrt(column_vals[j] * column_vals[j] + column_vals[j + 1] * column_vals[j + 1])
        cosine = column_vals[j] / radius
        sine_val = column_vals[j + 1] / radius
        rot_cos.append(cosine)
        rot_sin.append(sine_val)
        column_vals[j] = radius
        target[j + 1] = -sine_val * target[j]
        target[j] = cosine * target[j]
        triangle.append(column_vals[: j + 1])
    coeffs = [None] * steps_total
    for j in reversed(range(steps_total)):
        running = target[j]
        for k in range(j + 1, steps_total):
            running = running - triangle[k][j] * coeffs[k]
        coeffs[j] = running / triangle[j][j]
    return coeffs


def per_device(rhs_field, neighbors, nu_mean, nu_ripple, mass_coeff, eddy_coeff):
    block, nodes_own = rhs_field.shape
    harmonics = nu_ripple.shape[0]
    halo_width = IF
    harm_start = lax.axis_index("harm") * block
    kernel = nu_ripple.at[0].add(nu_mean)
    cos_table, sin_table = fourier_tables(harmonics)
    total_nodes = nodes_own * lax.axis_size("space")
    relative = jnp.mod(neighbors - lax.axis_index("space") * nodes_own, total_nodes)
    relative = jnp.where(relative >= total_nodes - halo_width, relative - total_nodes, relative)
    ext_index = relative + halo_width
    global_harm = harm_start + jnp.arange(block)
    harm_order = (global_harm // 2 + 1).astype(jnp.float32)
    sign_vals = jnp.where(global_harm % 2 == 0, 1.0, -1.0).astype(jnp.float32)
    factor = 4.0 * harm_order / harmonics * sign_vals
    node_share = nodes_own // lax.axis_size("harm")
    kernel_use = lax.dynamic_slice_in_dim(
        kernel, lax.axis_index("harm") * node_share, node_share, 2
    )
    kernel_flat = kernel_use.reshape(harmonics, -1)
    kernel_real = matmul_high(cos_table, kernel_flat)
    kernel_imag = -matmul_high(sin_table, kernel_flat)

    def convolve_spectrum(spec_real, spec_imag, out_cos, out_sin):
        prod_real = spec_real * kernel_real - spec_imag * kernel_imag
        prod_imag = spec_real * kernel_imag + spec_imag * kernel_real
        return (matmul_high(out_cos, prod_real) - matmul_high(out_sin, prod_imag)) / harmonics

    def operate(vector_in):
        extended = with_halo(vector_in, (("space", 1),), halo_width)
        gradients = extended[:, None, halo_width : halo_width + nodes_own] - extended[:, ext_index]
        spread = lax.all_to_all(gradients, "harm", split_axis=2, concat_axis=0, tiled=True)
        spread_flat = spread.reshape(harmonics, -1)
        spec_real = matmul_high(cos_table, spread_flat)
        spec_imag = -matmul_high(sin_table, spread_flat)
        fluxes = convolve_spectrum(spec_real, spec_imag, cos_table, sin_table)
        fluxes = fluxes.reshape(spread.shape)
        fluxes = lax.all_to_all(fluxes, "harm", split_axis=0, concat_axis=2, tiled=True)
        return (
            jnp.sum(fluxes, axis=1)
            + mass_coeff[None, :] * vector_in
            + eddy_coeff[None, :] * factor[:, None] * swap_pairs(vector_in)
        )

    beta_norm = jnp.sqrt(lax.psum(jnp.sum(rhs_field * rhs_field), ("harm", "space")))
    krylov = [rhs_field / beta_norm]
    columns = []
    for j in range(ITERS):
        image = operate(krylov[j])
        stacked = jnp.stack(krylov[: j + 1])
        local_dots = jnp.einsum("khn,hn->k", stacked, image, precision=lax.Precision.HIGHEST)
        projected, squared = lax.psum((local_dots, jnp.sum(image * image)), ("harm", "space"))
        image = image - jnp.einsum("k,khn->hn", projected, stacked, precision=lax.Precision.HIGHEST)
        length = jnp.sqrt(squared - jnp.sum(projected * projected))
        columns.append([projected[i] for i in range(j + 1)] + [length])
        if j + 1 < ITERS:
            krylov.append(image / length)
    coeffs = least_squares(columns, beta_norm)
    correction = coeffs[0] * krylov[0]
    for j in range(1, ITERS):
        correction = correction + coeffs[j] * krylov[j]
    residual = rhs_field - operate(correction)
    return (correction, residual)


def solution(mesh):
    return jax.shard_map(
        per_device,
        mesh=mesh,
        in_specs=(
            P("harm", "space"),
            P(None, "space"),
            P(None, "space"),
            P(None, None, "space"),
            P("space"),
            P("space"),
        ),
        out_specs=(P("harm", "space"), P("harm", "space")),
        check_vma=False,
    )
```

profile of v0, /device:TPU:0, one launch (start us, length us, event | category | flops | bytes accessed | tf_op | source)
XLA Modules:
  0.0 755.3 jit_solution(3855624070532140913)
XLA Ops:
  2.0 42.2 %psum.119 = f32[]{:T(128)} all-reduce(f32[]{:T(128)} %multiply_reduce_fusion.9), channel_id=1, replica_groups=mesh['harm'=2,'space'=16] {'harm','space'}, use_global_device_ids=true, to_apply=%region_1.2 | all-reduce | flops 1 | bytes 8 | tf_op jit(solution)/shard_map/psum | solution.py:112
  45.6 4.4 collective-permute-start.1
  51.7 5.5 gather_fusion
  58.9 3.5 all-to-all-start
  63.0 5.1 all-to-all-done
  73.8 3.4 all-to-all-start.1
  77.5 4.9 all-to-all-done.1
  83.9 39.0 %all-reduce.7 = (f32[]{:T(128)}, f32[1]{0:T(128)}) all-reduce(f32[]{:T(128)} %get-tuple-element.21, f32[1]{0:T(128)} %bitcast.7), channel_id=1, replica_groups=mesh['harm'=2,'space'=16] {'harm','space'}, use_global_device_ids=true, to_apply=%region_5.6 | all-reduce | flops 2 | bytes 16 | tf_op jit(solution)/shard_map/psum | solution.py:119
  126.3 4.4 collective-permute-start.3
  132.4 5.5 gather_fusion.1
  138.9 8.7 %all_to_all.216 = f32[2,1,32768]{2,1,0:T(1,128)S(1)} all-to-all(f32[2,1,32768]{2,1,0:T(1,128)S(1)} %reshape.388), channel_id=1, replica_groups=mesh['harm'=2,'space'=16] {'harm'}, dimensions={0} | all-to-all | bytes 524288 | tf_op jit(solution)/shard_map/all_to_all | solution.py:99
  147.6 1.4 reduce.32
  152.9 3.4 all-to-all-start.3
  156.6 4.9 all-to-all-done.3
  163.6 38.6 %all-reduce.6 = (f32[2]{0:T(128)S(1)}, f32[]{:T(128)}) all-reduce(f32[2]{0:T(128)S(1)} %convolution_bitcast_fusion.6, f32[]{:T(128)} %get-tuple-element.66), channel_id=1, replica_groups=mesh['harm'=2,'space'=16] {'harm','space'}, use_global_device_ids=true, to_apply=%region_7.8 | all-reduce | flops 3 | bytes 24 | tf_op jit(solution)/shard_map/psum | solution.py:119
  205.5 4.4 collective-permute-start.5
  211.6 5.5 gather_fusion.2
  218.1 8.5 %all_to_all.217 = f32[2,1,32768]{2,1,0:T(1,128)S(1)} all-to-all(f32[2,1,32768]{2,1,0:T(1,128)S(1)} %reshape.390), channel_id=1, replica_groups=mesh['harm'=2,'space'=16] {'harm'}, dimensions={0} | all-to-all | bytes 524288 | tf_op jit(solution)/shard_map/all_to_all | solution.py:99
  226.6 1.4 reduce.33
  231.9 3.4 all-to-all-start.5
  235.6 4.9 all-to-all-done.5
  242.5 39.2 %all-reduce.5 = (f32[3]{0:T(128)S(1)}, f32[]{:T(128)}) all-reduce(f32[3]{0:T(128)S(1)} %convolution_bitcast_fusion.5, f32[]{:T(128)} %get-tuple-element.64), channel_id=1, replica_groups=mesh['harm'=2,'space'=16] {'harm','space'}, use_global_device_ids=true, to_apply=%region_12.13 | all-reduce | flops 4 | bytes 32 | tf_op jit(solution)/shard_map/psum | solution.py:119
  285.0 4.4 collective-permute-start.7
  291.1 5.5 gather_fusion.3
  297.7 8.5 %all_to_all.218 = f32[2,1,32768]{2,1,0:T(1,128)S(1)} all-to-all(f32[2,1,32768]{2,1,0:T(1,128)S(1)} %reshape.392), channel_id=1, replica_groups=mesh['harm'=2,'space'=16] {'harm'}, dimensions={0} | all-to-all | bytes 524288 | tf_op jit(solution)/shard_map/all_to_all | solution.py:99
  306.2 1.4 reduce.34
  311.4 3.4 all-to-all-start.7
  315.2 4.9 all-to-all-done.7
  322.2 38.8 %all-reduce.4 = (f32[4]{0:T(128)S(1)}, f32[]{:T(128)}) all-reduce(f32[4]{0:T(128)S(1)} %convolution_bitcast_fusion.4, f32[]{:T(128)} %get-tuple-element.62), channel_id=1, replica_groups=mesh['harm'=2,'space'=16] {'harm','space'}, use_global_device_ids=true, to_apply=%region_17.18 | all-reduce | flops 5 | bytes 40 | tf_op jit(solution)/shard_map/psum | solution.py:119
  364.1 4.4 collective-permute-start.9
  370.2 5.5 gather_fusion.4
  377.4 3.7 all-to-all-start.8
  381.4 5.3 all-to-all-done.8
  386.7 1.4 reduce.35
  392.0 3.4 all-to-all-start.9
  395.4 5.1 all-to-all-done.9
  402.7 38.7 %all-reduce.3 = (f32[5]{0:T(128)S(1)}, f32[]{:T(128)}) all-reduce(f32[5]{0:T(128)S(1)} %convolution_bitcast_fusion.3, f32[]{:T(128)} %get-tuple-element.60), channel_id=1, replica_groups=mesh['harm'=2,'space'=16] {'harm','space'}, use_global_device_ids=true, to_apply=%region_22.23 | all-reduce | flops 6 | bytes 48 | tf_op jit(solution)/shard_map/psum | solution.py:119
  444.4 4.4 collective-permute-start.11
  450.5 5.5 gather_fusion.5
  457.7 3.5 all-to-all-start.10
  461.5 5.4 all-to-all-done.10
  466.8 1.4 reduce.36
  472.1 3.4 all-to-all-start.11
  475.5 5.1 all-to-all-done.11
  482.1 38.9 %all-reduce.2 = (f32[6]{0:T(128)S(1)}, f32[]{:T(128)}) all-reduce(f32[6]{0:T(128)S(1)} %convolution_bitcast_fusion.2, f32[]{:T(128)} %get-tuple-element.58), channel_id=1, replica_groups=mesh['harm'=2,'space'=16] {'harm','space'}, use_global_device_ids=true, to_apply=%region_27.28 | all-reduce | flops 7 | bytes 56 | tf_op jit(solution)/shard_map/psum | solution.py:119
  524.1 4.4 collective-permute-start.13
  530.2 5.5 gather_fusion.6
  537.4 3.5 all-to-all-start.12
  547.4 1.4 reduce.37
  552.7 3.4 all-to-all-start.13
  556.1 5.6 all-to-all-done.13
  563.2 38.0 %all-reduce.1 = (f32[7]{0:T(128)S(1)}, f32[]{:T(128)}) all-reduce(f32[7]{0:T(128)S(1)} %convolution_bitcast_fusion.1, f32[]{:T(128)} %get-tuple-element.56), channel_id=1, replica_groups=mesh['harm'=2,'space'=16] {'harm','space'}, use_global_device_ids=true, to_apply=%region_32.33 | all-reduce | flops 8 | bytes 64 | tf_op jit(solution)/shard_map/psum | solution.py:119
  604.4 4.4 collective-permute-start.15
  613.8 5.5 gather_fusion.7
  621.0 3.8 all-to-all-start.14
  637.9 1.4 reduce.38
  643.2 3.5 all-to-all-start.15
  666.3 39.5 %all-reduce = (f32[8]{0:T(128)S(1)}, f32[]{:T(128)}) all-reduce(f32[8]{0:T(128)S(1)} %convolution_bitcast_fusion, f32[]{:T(128)} %get-tuple-element.38), channel_id=1, replica_groups=mesh['harm'=2,'space'=16] {'harm','space'}, use_global_device_ids=true, to_apply=%region_37.38 | all-reduce | flops 9 | bytes 72 | tf_op jit(solution)/shard_map/psum | solution.py:119
  719.0 4.4 collective-permute-start.17
  725.1 5.5 gather_fusion.8
  731.7 8.5 %all_to_all.219 = f32[2,1,32768]{2,1,0:T(1,128)S(1)} all-to-all(f32[2,1,32768]{2,1,0:T(1,128)S(1)} %reshape.402), channel_id=1, replica_groups=mesh['harm'=2,'space'=16] {'harm'}, dimensions={0} | all-to-all | bytes 524288 | tf_op jit(solution)/shard_map/all_to_all | solution.py:99
  740.2 1.4 reduce.39
  745.5 3.4 all-to-all-start.17
  749.2 4.9 all-to-all-done.17
  (295 shorter events, 100.0 us)
Async XLA Ops:
  0.6 0.8 copy-start.3
  0.6 49.4 %copy-start = (f32[64,8,256]{2,1,0:T(8,128)S(1)}, f32[64,8,256]{2,1,0:T(8,128)}, u32[]{:S(2)}) copy-start(f32[64,8,256]{2,1,0:T(8,128)} %param.11) | copy-start | bytes 1572868
  45.6 4.4 copy-start.16
  45.6 5.9 collective-permute-start
  45.6 5.9 collective-permute-start.1
  50.0 0.7 copy-start.15
  58.9 9.1 %all-to-all-start = ((f32[2,1,32768]{2,1,0:T(1,128)}), f32[2,1,32768]{2,1,0:T(1,128)S(1)}, u32[]{:S(2)}, u32[]{:S(2)}) async-start(f32[2,1,32768]{2,1,0:T(1,128)} %reshape.386), calls=%async_computation | async-start | bytes 524288 | tf_op jit(solution)/shard_map/all_to_all | solution.py:99
  73.8 8.6 %all-to-all-start.1 = ((f32[64,8,128]{2,1,0:T(8,128)}), f32[64,8,128]{2,1,0:T(8,128)S(1)}, u32[]{:S(2)}, u32[]{:S(2)}) async-start(f32[64,8,128]{2,1,0:T(8,128)} %bitcast.171), calls=%async_computation.1 | async-start | bytes 524288 | tf_op jit(solution)/shard_map/all_to_all | solution.py:105
  77.5 5.0 copy-start.6
  82.4 0.7 copy-start.5
  82.5 0.7 copy-start.4
  126.2 5.9 collective-permute-start.2
  126.3 5.9 collective-permute-start.3
  152.9 8.6 %all-to-all-start.3 = ((f32[64,8,128]{2,1,0:T(8,128)}), f32[64,8,128]{2,1,0:T(8,128)S(1)}, u32[]{:S(2)}, u32[]{:S(2)}) async-start(f32[64,8,128]{2,1,0:T(8,128)} %bitcast.176), calls=%async_computation.3 | async-start | bytes 524288 | tf_op jit(solution)/shard_map/all_to_all | solution.py:105
  161.6 0.6 copy-start.7
  202.2 0.6 copy-start.17
  205.5 5.9 collective-permute-start.4
  205.5 5.9 collective-permute-start.5
  231.9 8.6 %all-to-all-start.5 = ((f32[64,8,128]{2,1,0:T(8,128)}), f32[64,8,128]{2,1,0:T(8,128)S(1)}, u32[]{:S(2)}, u32[]{:S(2)}) async-start(f32[64,8,128]{2,1,0:T(8,128)} %bitcast.181), calls=%async_computation.5 | async-start | bytes 524288 | tf_op jit(solution)/shard_map/all_to_all | solution.py:105
  240.6 0.6 copy-start.8
  281.8 0.5 copy-start.13
  285.0 5.9 collective-permute-start.6
  285.0 5.9 collective-permute-start.7
  311.4 8.6 %all-to-all-start.7 = ((f32[64,8,128]{2,1,0:T(8,128)}), f32[64,8,128]{2,1,0:T(8,128)S(1)}, u32[]{:S(2)}, u32[]{:S(2)}) async-start(f32[64,8,128]{2,1,0:T(8,128)} %bitcast.186), calls=%async_computation.7 | async-start | bytes 524288 | tf_op jit(solution)/shard_map/all_to_all | solution.py:105
  320.1 0.6 copy-start.9
  360.9 0.6 copy-start.11
  364.1 5.9 collective-permute-start.8
  364.1 5.9 collective-permute-start.9
  377.4 9.3 %all-to-all-start.8 = ((f32[2,1,32768]{2,1,0:T(1,128)}), f32[2,1,32768]{2,1,0:T(1,128)S(1)}, u32[]{:S(2)}, u32[]{:S(2)}) async-start(f32[2,1,32768]{2,1,0:T(1,128)} %reshape.394), calls=%async_computation.8 | async-start | bytes 524288 | tf_op jit(solution)/shard_map/all_to_all | solution.py:99
  392.0 8.6 %all-to-all-start.9 = ((f32[64,8,128]{2,1,0:T(8,128)}), f32[64,8,128]{2,1,0:T(8,128)S(1)}, u32[]{:S(2)}, u32[]{:S(2)}) async-start(f32[64,8,128]{2,1,0:T(8,128)} %bitcast.191), calls=%async_computation.9 | async-start | bytes 524288 | tf_op jit(solution)/shard_map/all_to_all | solution.py:105
  400.7 0.6 copy-start.10
  444.4 5.9 collective-permute-start.10
  444.4 5.9 collective-permute-start.11
  457.7 9.1 %all-to-all-start.10 = ((f32[2,1,32768]{2,1,0:T(1,128)}), f32[2,1,32768]{2,1,0:T(1,128)S(1)}, u32[]{:S(2)}, u32[]{:S(2)}) async-start(f32[2,1,32768]{2,1,0:T(1,128)} %reshape.396), calls=%async_computation.10 | async-start | bytes 524288 | tf_op jit(solution)/shard_map/all_to_all | solution.py:99
  472.1 8.6 %all-to-all-start.11 = ((f32[64,8,128]{2,1,0:T(8,128)}), f32[64,8,128]{2,1,0:T(8,128)S(1)}, u32[]{:S(2)}, u32[]{:S(2)}) async-start(f32[64,8,128]{2,1,0:T(8,128)} %bitcast.196), calls=%async_computation.11 | async-start | bytes 524288 | tf_op jit(solution)/shard_map/all_to_all | solution.py:105
  524.1 5.9 collective-permute-start.12
  524.1 5.9 collective-permute-start.13
  537.4 10.0 %all-to-all-start.12 = ((f32[2,1,32768]{2,1,0:T(1,128)}), f32[2,1,32768]{2,1,0:T(1,128)S(1)}, u32[]{:S(2)}, u32[]{:S(2)}) async-start(f32[2,1,32768]{2,1,0:T(1,128)} %reshape.398), calls=%async_computation.12 | async-start | bytes 524288 | tf_op jit(solution)/shard_map/all_to_all | solution.py:99
  543.0 0.7 copy-start.18
  552.7 9.0 %all-to-all-start.13 = ((f32[64,8,128]{2,1,0:T(8,128)}), f32[64,8,128]{2,1,0:T(8,128)S(1)}, u32[]{:S(2)}, u32[]{:S(2)}) async-start(f32[64,8,128]{2,1,0:T(8,128)} %bitcast.201), calls=%async_computation.13 | async-start | bytes 524288 | tf_op jit(solution)/shard_map/all_to_all | solution.py:105
  604.4 4.4 copy-start.14
  604.4 9.2 %collective-permute-start.14 = (f32[32,64]{1,0:T(8,128)S(1)}, f32[32,64]{1,0:T(8,128)S(1)}, u32[]{:S(2)}, u32[]{:S(2)}) collective-permute-start(f32[32,64]{1,0:T(8,128)S(1)} %get-tuple-element.71), channel_id=1, source_target_pairs={{0,1},{1,2},{2,3},{3,4},{4,5},{5,6},{6,7},{7,8},{8,9},{9,10},{10,1... | collective-permute-start | bytes 24584 | tf_op jit(solution)/shard_map/ppermute | solution.py:17
  604.4 9.2 %collective-permute-start.15 = (f32[32,64]{1,0:T(8,128)S(1)}, f32[32,64]{1,0:T(8,128)S(1)}, u32[]{:S(2)}, u32[]{:S(2)}) collective-permute-start(f32[32,64]{1,0:T(8,128)S(1)} %get-tuple-element.72), channel_id=1, source_target_pairs={{1,0},{2,1},{3,2},{4,3},{5,4},{6,5},{7,6},{8,7},{9,8},{10,9},{11,1... | collective-permute-start | bytes 24584 | tf_op jit(solution)/shard_map/ppermute | solution.py:18
  619.9 4.9 copy-start.12
  621.0 16.8 %all-to-all-start.14 = ((f32[2,1,32768]{2,1,0:T(1,128)}), f32[2,1,32768]{2,1,0:T(1,128)S(1)}, u32[]{:S(2)}, u32[]{:S(2)}) async-start(f32[2,1,32768]{2,1,0:T(1,128)} %reshape.400), calls=%async_computation.14 | async-start | bytes 524288 | tf_op jit(solution)/shard_map/all_to_all | solution.py:99
  643.2 21.6 %all-to-all-start.15 = ((f32[64,8,128]{2,1,0:T(8,128)}), f32[64,8,128]{2,1,0:T(8,128)S(1)}, u32[]{:S(2)}, u32[]{:S(2)}) async-start(f32[64,8,128]{2,1,0:T(8,128)} %bitcast.206), calls=%async_computation.15 | async-start | bytes 524288 | tf_op jit(solution)/shard_map/all_to_all | solution.py:105
  664.6 1.0 copy-start.2
  718.9 35.2 %copy-start.1 = (f32[32,256]{1,0:T(8,128)}, f32[32,256]{1,0:T(8,128)S(1)}, u32[]{:S(2)}) copy-start(f32[32,256]{1,0:T(8,128)S(1)} %multiply_add_fusion) | copy-start | bytes 98308
  719.0 5.9 collective-permute-start.16
  719.0 5.9 collective-permute-start.17
  745.5 8.6 %all-to-all-start.17 = ((f32[64,8,128]{2,1,0:T(8,128)}), f32[64,8,128]{2,1,0:T(8,128)S(1)}, u32[]{:S(2)}, u32[]{:S(2)}) async-start(f32[64,8,128]{2,1,0:T(8,128)} %bitcast.211), calls=%async_computation.17 | async-start | bytes 524288 | tf_op jit(solution)/shard_map/all_to_all | solution.py:105
where the time goes:
time: 765 us; the launch traced here: 755 us
  blocking collectives  387 us (51%)
  starting transfers between devices  89.1 us (12%)
  local copies, waits for them, and re-layouts  86.9 us (11%)
  waiting for transfers between devices  65.6 us (9%)
  between operations  62.1 us (8%)
  other arithmetic  36.7 us (5%)
  matrix products  27.6 us (4%)
    psum x8, blocking collectives, per_device(): lax.psum((local_dots, jnp.sum(image * image)), ('harm', 'space'))  311 us
    gather x9, local copies, waits for them, and re-layouts, operate(): extended[:, ext_index]  49.2 us
    psum x1, blocking collectives, per_device(): lax.psum(jnp.sum(rhs_field * rhs_field), ('harm', 'space'))  42.2 us
    all_to_all x9, waiting for transfers between devices, operate(): lax.all_to_all(fluxes, 'harm', split_axis=0, concat_axis=2, tiled=True)  40.4 us
    ppermute x9, starting transfers between devices, with_halo(): after = lax.ppermute(leading, axis, down)  40 us
    all_to_all x4, blocking collectives, operate(): lax.all_to_all(gradients, 'harm', split_axis=2, concat_axis=0, tiled=True)  34.3 us
    all_to_all x9, starting transfers between devices, operate(): lax.all_to_all(fluxes, 'harm', split_axis=0, concat_axis=2, tiled=True)  31 us
    unnamed x71, local copies, waits for them, and re-layouts  24.3 us
  transfers between devices with their start and end apart: 32, of which 18 were waited for; matrix products, arithmetic and copies ran while one was open for 1% of the time, Pallas kernels for 0%

commit v1 on v0

v1 whole, which is shorter than its diff:
```python
import functools

import jax
import jax.numpy as jnp
import ml_dtypes
import numpy as np
from jax import lax
from jax.experimental import pallas as pl
from jax.experimental.pallas import tpu as pltpu
from jax.sharding import PartitionSpec as P

IF = 64
ITERS = 8
MESH = pl.DeviceIdType.MESH


def tables(harmonics):
    half = harmonics // 2
    index = np.arange(harmonics)
    phase = 2.0 * np.pi * ((index[:, None] * index[None, :]) % harmonics) / harmonics
    plain = np.concatenate([np.cos(phase[:half]), -np.sin(phase[:half])], axis=0)
    plain[half] = np.cos(phase[half])
    scale = np.full((harmonics, 1), np.sqrt(2.0 / harmonics))
    scale[0] = scale[half] = np.sqrt(1.0 / harmonics)
    unitary = plain * scale
    swap = np.zeros((harmonics, harmonics))
    swap[index, index ^ 1] = 4.0 * (index // 2 + 1) / harmonics * np.where(index % 2 == 0, 1.0, -1.0)
    swap = unitary @ swap @ unitary.T
    high = swap.astype(np.float32).astype(ml_dtypes.bfloat16)
    low = (swap - high.astype(np.float64)).astype(ml_dtypes.bfloat16)
    swap_parts = np.concatenate([high, low, high, low], axis=1)
    return plain.astype(np.float32), unitary.astype(np.float32), unitary.T.astype(np.float32), swap_parts


def split_parts(value, count):
    parts = []
    for _ in range(count):
        part = value.astype(jnp.bfloat16)
        parts.append(part)
        value = value - part.astype(jnp.float32)
    return parts


def dot_high(left, right):
    return jnp.dot(left, right, precision=lax.Precision.HIGHEST, preferred_element_type=jnp.float32)


def solve_least_squares(columns, beta):
    steps = len(columns)
    rot_cos, rot_sin = [], []
    target = [beta] + [None] * steps
    triangle = []
    for j in range(steps):
        col = list(columns[j])
        for i in range(j):
            first, second = col[i], col[i + 1]
            col[i] = rot_cos[i] * first + rot_sin[i] * second
            col[i + 1] = rot_cos[i] * second - rot_sin[i] * first
        radius = jnp.sqrt(col[j] * col[j] + col[j + 1] * col[j + 1])
        cosine, sine = col[j] / radius, col[j + 1] / radius
        rot_cos.append(cosine)
        rot_sin.append(sine)
        col[j] = radius
        target[j + 1] = -sine * target[j]
        target[j] = cosine * target[j]
        triangle.append(col[: j + 1])
    coeffs = [None] * steps
    for j in reversed(range(steps)):
        running = target[j]
        for k in range(j + 1, steps):
            running = running - triangle[k][j] * coeffs[k]
        coeffs[j] = running / triangle[j][j]
    return coeffs


def gmres_kernel(
    n_harm, n_space,
    rhs_ref, nbr_ref, mean_ref, rip_ref, mass_ref, eddy_ref,
    plain_ref, unit_ref, unit_t_ref, swap_ref,
    corr_ref, res_ref,
    rhs_all, onehot, k_re, k_re2, k_im, basis, image, field, halo, msg, dots_in, phys, phys_in,
    rhs_send, rhs_recv, halo_send, halo_recv, dot_send, dot_recv, out_send, out_recv,
):
    block, own2 = rhs_ref.shape
    own = own2 // 2
    harmonics = rip_ref.shape[0]
    half = harmonics // 2
    degree = nbr_ref.shape[0]
    group = n_harm // 2
    places = 2 * n_space
    h = lax.axis_index("harm")
    s = lax.axis_index("space")
    lane_rank = lax.rem(h, group)

    def side_of(harm, space):
        return lax.rem(harm // group + space, 2)

    side = side_of(h, s)
    place = 2 * s + side

    def device_at(position):
        space = position // 2
        return (lax.rem(lax.rem(position, 2) + space, 2) * group + lane_rank, space)

    def lanes(which):
        return pl.ds(pl.multiple_of(which * own, own), own)

    def rows(which):
        return pl.ds(pl.multiple_of(which * block, block), block)

    barrier = pltpu.get_barrier_semaphore()

    def greet(offset, carry):
        pl.semaphore_signal(barrier, inc=1, device_id=device_at(lax.rem(place + offset, places)), device_id_type=MESH)
        return carry

    lax.fori_loop(1, places, greet, 0)
    extra = [o for o in range(1, n_harm) if o % group != 0]
    for o in extra:
        pl.semaphore_signal(barrier, inc=1, device_id=(lax.rem(h + o, n_harm), s), device_id_type=MESH)
    pl.semaphore_wait(barrier, places - 1 + len(extra))

    rhs_copies = []
    for o in range(1, n_harm):
        peer = lax.rem(h + o, n_harm)
        copy = pltpu.make_async_remote_copy(
            src_ref=rhs_ref.at[:, lanes(side_of(peer, s))],
            dst_ref=rhs_all.at[rows(h)],
            send_sem=rhs_send.at[o - 1],
            recv_sem=rhs_recv.at[o - 1],
            device_id=(peer, s),
            device_id_type=MESH,
        )
        copy.start()
        rhs_copies.append(copy)
    rhs_all[rows(h)] = rhs_ref[:, lanes(side)]

    first_row = lax.broadcasted_iota(jnp.int32, (half, own), 0) == 0
    row_index = lax.broadcasted_iota(jnp.int32, (own2, own), 0)
    start = place * own
    for d in range(degree):
        spectrum = dot_high(plain_ref[...], rip_ref[:, d, lanes(side)])
        mean = mean_ref[d : d + 1, lanes(side)]
        real, imag = spectrum[:half], spectrum[half:]
        k_re[d] = real + mean
        k_re2[d] = jnp.where(first_row, imag, real) + mean
        k_im[d] = jnp.where(first_row, 0.0, imag)
        spot = jnp.bitwise_and(nbr_ref[d : d + 1, lanes(side)] - start, own2 - 1)
        onehot[:, d * own : (d + 1) * own] = jnp.where(row_index == spot, 1.0, 0.0).astype(jnp.bfloat16)
    mass = mass_ref[:, lanes(side)]
    eddy = eddy_ref[:, lanes(side)]
    for copy in rhs_copies:
        copy.wait_recv()

    lane_index = lax.broadcasted_iota(jnp.int32, (1, 128), 1)
    near = lax.broadcasted_iota(jnp.int32, (harmonics, own), 1) < IF
    left = device_at(lax.rem(place + places - 1, places))
    right = device_at(lax.rem(place + 1, places))
    halo_copies = []

    def send_halo(k, source):
        for way, target in ((0, right), (1, left)):
            copy = pltpu.make_async_remote_copy(
                src_ref=source,
                dst_ref=halo.at[k, way],
                send_sem=halo_send.at[k, way],
                recv_sem=halo_recv.at[k, way],
                device_id=target,
                device_id_type=MESH,
            )
            copy.start()
            halo_copies.append(copy)

    def operate(k, vector):
        mine = split_parts(vector, 3)
        swapped = jnp.dot(
            swap_ref[...], jnp.concatenate([mine[0], mine[0], mine[1], mine[1]], axis=0),
            preferred_element_type=jnp.float32,
        )
        total = mass * vector + eddy * swapped
        halo_copies[2 * k].wait_recv()
        halo_copies[2 * k + 1].wait_recv()
        outer = split_parts(jnp.where(near, halo[k, 1], halo[k, 0]), 3)
        stacked = jnp.concatenate(
            [jnp.concatenate([a, b], axis=1) for a, b in zip(mine, outer)], axis=0
        )
        v_re, v_im = vector[:half], vector[half:]
        sum_re, sum_im = total[:half], total[half:]
        for d in range(0, degree, 2):
            far = jnp.dot(stacked, onehot[:, d * own : (d + 2) * own], preferred_element_type=jnp.float32)
            far = far[:harmonics] + far[harmonics : 2 * harmonics] + far[2 * harmonics :]
            for e in range(2):
                g_re = v_re - far[:half, e * own : (e + 1) * own]
                g_im = v_im - far[half:, e * own : (e + 1) * own]
                sum_re += k_re[d + e] * g_re - k_im[d + e] * g_im
                sum_im += k_re2[d + e] * g_im + k_im[d + e] * g_re
        return jnp.concatenate([sum_re, sum_im], axis=0)

    def total_of(product):
        return jnp.sum(jnp.sum(product, axis=0, keepdims=True), axis=1, keepdims=True)

    def send_dots(k, products):
        row = jnp.zeros((1, 128), jnp.float32)
        for i, product in enumerate(products):
            row = jnp.where(lane_index == i, total_of(product), row)
        msg[k] = row

        def send(offset, carry):
            pltpu.make_async_remote_copy(
                src_ref=msg.at[k],
                dst_ref=dots_in.at[k, offset - 1],
                send_sem=dot_send.at[k],
                recv_sem=dot_recv.at[k],
                device_id=device_at(lax.rem(place + offset, places)),
                device_id_type=MESH,
            ).start()
            return carry

        lax.fori_loop(1, places, send, 0)

    def wait_dots(sem, k):
        pltpu.make_async_copy(dots_in.at[k], dots_in.at[k], sem.at[k]).wait()

    def receive_dots(k, count):
        wait_dots(dot_recv, k)
        row = msg[k] + jnp.sum(dots_in[k], axis=0)
        return [row[:, i : i + 1] for i in range(count)]

    field[0] = dot_high(unit_ref[...], rhs_all[...])
    send_halo(0, field.at[0])
    rhs = field[0]
    rhs_image = operate(0, rhs)
    field[1] = rhs_image
    send_halo(1, field.at[1])
    send_dots(0, [rhs * rhs, rhs * rhs_image, rhs_image * rhs_image])
    second = operate(1, rhs_image)
    rr, ru, uu = receive_dots(0, 3)
    beta = jnp.sqrt(rr)
    theta = ru / rr
    inverse = 1.0 / beta
    length = jnp.sqrt((uu - ru * theta) / rr)
    basis[0] = rhs * inverse
    image[0] = (rhs_image - theta * rhs) * inverse
    shifted = (second - theta * rhs_image) * inverse - theta * image[0]
    columns = [[theta, length]]
    basis[1] = image[0] / length
    image[1] = shifted / length
    for j in range(1, ITERS):
        current = image[j]
        if j + 1 < ITERS:
            send_halo(j + 1, image.at[j])
        send_dots(j, [basis[i] * current for i in range(j + 1)] + [current * current])
        if j + 1 < ITERS:
            following = operate(j + 1, current) - theta * current
        found = receive_dots(j, j + 2)
        dots, squared = found[: j + 1], found[j + 1]
        for value in dots:
            squared = squared - value * value
        length = jnp.sqrt(squared)
        columns.append(dots[:j] + [dots[j] + theta, length])
        if j + 1 < ITERS:
            scale = 1.0 / length
            for i, value in enumerate(dots):
                current = current - value * basis[i]
                following = following - value * image[i]
            basis[j + 1] = current * scale
            image[j + 1] = following * scale
    coeffs = solve_least_squares(columns, beta)
    correction = coeffs[0] * basis[0]
    product = coeffs[0] * image[0]
    for j in range(1, ITERS):
        correction = correction + coeffs[j] * basis[j]
        product = product + coeffs[j] * image[j]
    residual = rhs - product - theta * correction
    phys[0] = dot_high(unit_t_ref[...], correction)
    phys[1] = dot_high(unit_t_ref[...], residual)

    other = lax.rem(h + group, n_harm)
    final = pltpu.make_async_remote_copy(
        src_ref=phys.at[:, rows(other)],
        dst_ref=phys_in,
        send_sem=out_send,
        recv_sem=out_recv,
        device_id=(other, s),
        device_id_type=MESH,
    )
    final.start()
    corr_ref[:, lanes(side)] = phys[0, rows(h)]
    res_ref[:, lanes(side)] = phys[1, rows(h)]
    for copy in rhs_copies + halo_copies:
        copy.wait_send()
    for k in range(ITERS):
        wait_dots(dot_send, k)
    final.wait()
    corr_ref[:, lanes(1 - side)] = phys_in[0]
    res_ref[:, lanes(1 - side)] = phys_in[1]


def per_device(n_harm, n_space, rhs_field, neighbors, nu_mean, nu_ripple, mass_coeff, eddy_coeff):
    block, own2 = rhs_field.shape
    own = own2 // 2
    harmonics, degree = nu_ripple.shape[:2]
    plain, unit, unit_t, swap_parts = tables(harmonics)
    places = 2 * n_space
    f32 = jnp.float32
    vmem = pl.BlockSpec(memory_space=pltpu.VMEM)
    dma = pltpu.SemaphoreType.DMA
    return pl.pallas_call(
        functools.partial(gmres_kernel, n_harm, n_space),
        out_shape=(jax.ShapeDtypeStruct((block, own2), f32),) * 2,
        in_specs=[vmem] * 10,
        out_specs=(vmem, vmem),
        scratch_shapes=[
            pltpu.VMEM((harmonics, own), f32),
            pltpu.VMEM((own2, degree * own), jnp.bfloat16),
            pltpu.VMEM((degree, harmonics // 2, own), f32),
            pltpu.VMEM((degree, harmonics // 2, own), f32),
            pltpu.VMEM((degree, harmonics // 2, own), f32),
            pltpu.VMEM((ITERS, harmonics, own), f32),
            pltpu.VMEM((ITERS, harmonics, own), f32),
            pltpu.VMEM((2, harmonics, own), f32),
            pltpu.VMEM((ITERS, 2, harmonics, own), f32),
            pltpu.VMEM((ITERS, 1, 128), f32),
            pltpu.VMEM((ITERS, places - 1, 1, 128), f32),
            pltpu.VMEM((2, harmonics, own), f32),
            pltpu.VMEM((2, block, own), f32),
            dma((n_harm - 1,)),
            dma((n_harm - 1,)),
            dma((ITERS, 2)),
            dma((ITERS, 2)),
            dma((ITERS,)),
            dma((ITERS,)),
            dma,
            dma,
        ],
        compiler_params=pltpu.CompilerParams(
            collective_id=0, has_side_effects=True, vmem_limit_bytes=32 * 1024 * 1024
        ),
    )(
        rhs_field, neighbors, nu_mean, nu_ripple,
        mass_coeff.reshape(1, own2), eddy_coeff.reshape(1, own2),
        jnp.asarray(plain), jnp.asarray(unit), jnp.asarray(unit_t), jnp.asarray(swap_parts),
    )


def solution(mesh):
    return jax.shard_map(
        functools.partial(per_device, mesh.shape["harm"], mesh.shape["space"]),
        mesh=mesh,
        in_specs=(
            P("harm", "space"),
            P(None, "space"),
            P(None, "space"),
            P(None, None, "space"),
            P("space"),
            P("space"),
        ),
        out_specs=(P("harm", "space"), P("harm", "space")),
        check_vma=False,
    )
```

time: 765 us -> 66.3 us (0.09); the launches traced: 755 us -> 65.7 us
  blocking collectives: 387 us -> 0 us
  starting transfers between devices: 89.1 us -> 0 us
  local copies, waits for them, and re-layouts: 86.9 us -> 8.13 us
  waiting for transfers between devices: 65.6 us -> 0 us
  between operations: 62.1 us -> 0.67 us
  Pallas kernels: 0 us -> 56.9 us
  other arithmetic: 36.7 us -> 0 us
  matrix products: 27.6 us -> 0 us
    psum x9 -> x0, blocking collectives: 353 us -> none  [the longest x8 311 us: per_device(): lax.psum((local_dots, jnp.sum(image * image)), ('harm', 'space'))]
    pallas_call x0 -> x1, Pallas kernels: none -> 56.9 us  [per_device(): pl.pallas_call(functools.partial(gmres_kernel, n_harm, n_space), out_shap...]
    all_to_all x14 -> x0, waiting for transfers between devices: 56.2 us -> none  [the longest x9 40.4 us: operate(): lax.all_to_all(fluxes, 'harm', split_axis=0, concat_axis=2, tiled=True)]
    gather x9 -> x0, local copies, waits for them, and re-layouts: 49.2 us -> none  [operate(): extended[:, ext_index]]
    all_to_all x14 -> x0, starting transfers between devices: 49.1 us -> none  [the longest x9 31 us: operate(): lax.all_to_all(fluxes, 'harm', split_axis=0, concat_axis=2, tiled=True)]
    ppermute x18 -> x0, starting transfers between devices: 40 us -> none  [the longest x9 40 us: with_halo(): after = lax.ppermute(leading, axis, down)]
    all_to_all x4 -> x0, blocking collectives: 34.3 us -> none  [operate(): lax.all_to_all(gradients, 'harm', split_axis=2, concat_axis=0, tiled=True)]
    dot_general x51 -> x0, matrix products: 27.6 us -> none  [the longest x38 20.3 us: matmul_high(): jnp.dot(left, right, precision=lax.Precision.HIGHEST, preferred_element_t...]
  transfers between devices with their start and end apart: 32 -> 0, of which waited for: 18 -> 0; matrix products, arithmetic and copies ran while one was open for 1% -> 0% of each run, Pallas kernels for 0% -> 0%
where the time goes in v1:
time: 66.3 us; the launch traced here: 65.7 us
  Pallas kernels  56.9 us (86%)
  local copies, waits for them, and re-layouts  8.13 us (12%)
  between operations  0.67 us (1%)
    pallas_call x1, Pallas kernels, per_device(): pl.pallas_call(functools.partial(gmres_kernel, n_harm, n_space), out_shap...  56.9 us
    unnamed x22, local copies, waits for them, and re-layouts  8.13 us

profile of v1, /device:TPU:0, one launch (start us, length us, event | category | flops | bytes accessed | tf_op | source)
XLA Modules:
  0.0 65.7 jit_solution(17942132501532480022)
XLA Ops:
  0.6 0.0 copy-start.9
  0.6 0.0 copy-start.8
  0.7 0.7 %copy-done.9 = f32[256]{0:T(256)S(1)} copy-done((f32[256]{0:T(256)S(1)}, f32[256]{0:T(256)}, u32[]{:S(2)}) %copy-start.9) | copy-done | bytes 1048
  1.3 0.0 copy-done.8
  1.3 0.0 copy-start
  1.3 1.0 %copy-done = f32[64,8,256]{2,1,0:T(8,128)S(1)} copy-done((f32[64,8,256]{2,1,0:T(8,128)S(1)}, f32[64,8,256]{2,1,0:T(8,128)}, u32[]{:S(2)}) %copy-start) | copy-done | bytes 524312
  2.4 0.0 copy-start.1
  2.4 0.8 %copy-done.1 = f32[32,256]{1,0:T(8,128)S(1)} copy-done((f32[32,256]{1,0:T(8,128)S(1)}, f32[32,256]{1,0:T(8,128)}, u32[]{:S(2)}) %copy-start.1) | copy-done | bytes 32792
  3.1 0.0 copy-start.2
  3.1 0.8 %copy-done.2 = bf16[64,256]{1,0:T(8,128)(2,1)S(1)} copy-done((bf16[64,256]{1,0:T(8,128)(2,1)S(1)}, bf16[64,256]{1,0:T(8,128)(2,1)}, u32[]{:S(2)}) %copy-start.2) | copy-done | bytes 32792
  3.9 0.0 copy-start.3
  3.9 0.8 %copy-done.3 = f32[64,64]{1,0:T(8,128)S(1)} copy-done((f32[64,64]{1,0:T(8,128)S(1)}, f32[64,64]{1,0:T(8,128)}, u32[]{:S(2)}) %copy-start.3) | copy-done | bytes 16408
  4.6 0.0 copy-start.4
  4.6 0.8 %copy-done.4 = f32[64,64]{1,0:T(8,128)S(1)} copy-done((f32[64,64]{1,0:T(8,128)S(1)}, f32[64,64]{1,0:T(8,128)}, u32[]{:S(2)}) %copy-start.4) | copy-done | bytes 16408
  5.4 0.0 copy-start.5
  5.4 0.8 %copy-done.5 = f32[64,64]{1,0:T(8,128)S(1)} copy-done((f32[64,64]{1,0:T(8,128)S(1)}, f32[64,64]{1,0:T(8,128)}, u32[]{:S(2)}) %copy-start.5) | copy-done | bytes 16408
  6.2 0.0 copy-start.6
  6.2 0.7 %copy-done.6 = s32[8,256]{1,0:T(8,128)S(1)} copy-done((s32[8,256]{1,0:T(8,128)S(1)}, s32[8,256]{1,0:T(8,128)}, u32[]{:S(2)}) %copy-start.6) | copy-done | bytes 8216
  6.9 0.0 copy-start.7
  6.9 0.7 %copy-done.7 = f32[8,256]{1,0:T(8,128)S(1)} copy-done((f32[8,256]{1,0:T(8,128)S(1)}, f32[8,256]{1,0:T(8,128)}, u32[]{:S(2)}) %copy-start.7) | copy-done | bytes 8216
  7.6 56.9 %shard_map.113 = (f32[32,256]{1,0:T(8,128)S(1)}, f32[32,256]{1,0:T(8,128)S(1)}) custom-call(f32[32,256]{1,0:T(8,128)S(1)} %copy-done.1, s32[8,256]{1,0:T(8,128)S(1)} %copy-done.6, f32[8,256]{1,0:T(8,128)S(1)} %copy-done.7, f32[64,8,256]{2,1,0:T(8,128)S(1)} %copy-done, f32[1,256]{1,0:T(1,128)S(1)} %bitcast.2, f32[1,256]{1,0:T(1,128)S(1)} %bitcast.3, ...), custom_call_target="tpu_custom_call" | custom-call | tf_op jit(solution)/shard_map/pallas_call | solution.py:308
  64.4 0.6 copy.14
  65.0 0.6 copy.15
Async XLA Ops:
  0.6 0.7 %copy-start.9 = (f32[256]{0:T(256)S(1)}, f32[256]{0:T(256)}, u32[]{:S(2)}) copy-start(f32[256]{0:T(256)} %param.15) | copy-start | bytes 3076
  0.6 0.7 %copy-start.8 = (f32[256]{0:T(256)S(1)}, f32[256]{0:T(256)}, u32[]{:S(2)}) copy-start(f32[256]{0:T(256)} %param.14) | copy-start | bytes 3076
  1.3 1.0 %copy-start = (f32[64,8,256]{2,1,0:T(8,128)S(1)}, f32[64,8,256]{2,1,0:T(8,128)}, u32[]{:S(2)}) copy-start(f32[64,8,256]{2,1,0:T(8,128)} %rip_ref.1) | copy-start | bytes 1572868
  2.4 0.8 %copy-start.1 = (f32[32,256]{1,0:T(8,128)S(1)}, f32[32,256]{1,0:T(8,128)}, u32[]{:S(2)}) copy-start(f32[32,256]{1,0:T(8,128)} %rhs_ref.1) | copy-start | bytes 98308
  3.1 0.8 %copy-start.2 = (bf16[64,256]{1,0:T(8,128)(2,1)S(1)}, bf16[64,256]{1,0:T(8,128)(2,1)}, u32[]{:S(2)}) copy-start(bf16[64,256]{1,0:T(8,128)(2,1)} %constant.11.clone.swap_ref) | copy-start | bytes 98308
  3.9 0.8 %copy-start.3 = (f32[64,64]{1,0:T(8,128)S(1)}, f32[64,64]{1,0:T(8,128)}, u32[]{:S(2)}) copy-start(f32[64,64]{1,0:T(8,128)} %constant.10.clone.unit_t_ref) | copy-start | bytes 49156
  4.6 0.8 %copy-start.4 = (f32[64,64]{1,0:T(8,128)S(1)}, f32[64,64]{1,0:T(8,128)}, u32[]{:S(2)}) copy-start(f32[64,64]{1,0:T(8,128)} %constant.9.clone.unit_ref) | copy-start | bytes 49156
  5.4 0.8 %copy-start.5 = (f32[64,64]{1,0:T(8,128)S(1)}, f32[64,64]{1,0:T(8,128)}, u32[]{:S(2)}) copy-start(f32[64,64]{1,0:T(8,128)} %constant.8.clone.plain_ref) | copy-start | bytes 49156
  6.2 0.7 %copy-start.6 = (s32[8,256]{1,0:T(8,128)S(1)}, s32[8,256]{1,0:T(8,128)}, u32[]{:S(2)}) copy-start(s32[8,256]{1,0:T(8,128)} %nbr_ref.1) | copy-start | bytes 24580
  6.9 0.7 %copy-start.7 = (f32[8,256]{1,0:T(8,128)S(1)}, f32[8,256]{1,0:T(8,128)}, u32[]{:S(2)}) copy-start(f32[8,256]{1,0:T(8,128)} %mean_ref.1) | copy-start | bytes 24580

commit v2 on v1

v2 whole, which is shorter than its diff:
```python
import functools

import jax
import jax.numpy as jnp
import ml_dtypes
import numpy as np
from jax import lax
from jax.experimental import pallas as pl
from jax.experimental.pallas import tpu as pltpu
from jax.sharding import PartitionSpec as P

IF = 64
ITERS = 8
MESH = pl.DeviceIdType.MESH


def tables(harmonics):
    half = harmonics // 2
    index = np.arange(harmonics)
    phase = 2.0 * np.pi * ((index[:, None] * index[None, :]) % harmonics) / harmonics
    plain = np.concatenate([np.cos(phase[:half]), -np.sin(phase[:half])], axis=0)
    plain[half] = np.cos(phase[half])
    scale = np.full((harmonics, 1), np.sqrt(2.0 / harmonics))
    scale[0] = scale[half] = np.sqrt(1.0 / harmonics)
    unitary = plain * scale
    swap = np.zeros((harmonics, harmonics))
    swap[index, index ^ 1] = 4.0 * (index // 2 + 1) / harmonics * np.where(index % 2 == 0, 1.0, -1.0)
    swap = unitary @ swap @ unitary.T
    high = swap.astype(np.float32).astype(ml_dtypes.bfloat16)
    low = (swap - high.astype(np.float64)).astype(ml_dtypes.bfloat16)
    swap_parts = np.concatenate([high, low, high, low], axis=1)
    return plain.astype(np.float32), unitary.astype(np.float32), unitary.T.astype(np.float32), swap_parts


def split_parts(value, count):
    parts = []
    for _ in range(count):
        part = value.astype(jnp.bfloat16)
        parts.append(part)
        value = value - part.astype(jnp.float32)
    return parts


def dot_high(left, right):
    return jnp.dot(left, right, precision=lax.Precision.HIGHEST, preferred_element_type=jnp.float32)


class LeastSquares:
    def __init__(self, beta):
        self.rotations = []
        self.triangle = []
        self.target = [beta]

    def add(self, column):
        col = list(column)
        for i, (cosine, sine) in enumerate(self.rotations):
            first, second = col[i], col[i + 1]
            col[i] = cosine * first + sine * second
            col[i + 1] = cosine * second - sine * first
        j = len(self.rotations)
        radius = jnp.sqrt(col[j] * col[j] + col[j + 1] * col[j + 1])
        cosine, sine = col[j] / radius, col[j + 1] / radius
        self.rotations.append((cosine, sine))
        col[j] = radius
        self.target.append(-sine * self.target[j])
        self.target[j] = cosine * self.target[j]
        self.triangle.append(col[: j + 1])

    def solve(self):
        steps = len(self.triangle)
        coeffs = [None] * steps
        for j in reversed(range(steps)):
            running = self.target[j]
            for k in range(j + 1, steps):
                running = running - self.triangle[k][j] * coeffs[k]
            coeffs[j] = running / self.triangle[j][j]
        return coeffs


def gmres_kernel(
    n_harm, n_space,
    rhs_ref, nbr_hbm, mean_hbm, rip_hbm, mass_hbm, eddy_hbm,
    plain_hbm, unit_hbm, unit_t_hbm, swap_hbm,
    corr_ref, res_ref,
    nbr_ref, mean_ref, rip_ref, mass_ref, eddy_ref, plain_ref, unit_ref, unit_t_ref, swap_ref, load_sem,
    cross_send, cross_recv,
    rhs_all, hot_own, hot_ghost, k_re, k_re2, k_im, basis, image, image2, field, halo, msg, dots_in, phys, phys_in,
    rhs_send, rhs_recv, halo_send, halo_recv, dot_send, dot_recv, out_send, out_recv,
):
    block, own2 = rhs_ref.shape
    own = own2 // 2
    harmonics = rip_hbm.shape[0]
    half = harmonics // 2
    degree = nbr_hbm.shape[0]
    group = n_harm // 2
    places = 2 * n_space
    h = lax.axis_index("harm")
    s = lax.axis_index("space")
    lane_rank = lax.rem(h, group)

    def side_of(harm, space):
        return lax.rem(harm // group + space, 2)

    side = side_of(h, s)
    place = 2 * s + side

    def device_at(position):
        space = position // 2
        return (lax.rem(lax.rem(position, 2) + space, 2) * group + lane_rank, space)

    def lanes(which):
        return pl.ds(pl.multiple_of(which * own, own), own)

    def rows(which):
        return pl.ds(pl.multiple_of(which * block, block), block)

    edge_data = (
        (nbr_hbm, nbr_ref), (mean_hbm, mean_ref), (mass_hbm, mass_ref), (rip_hbm, rip_ref), (eddy_hbm, eddy_ref)
    )
    loads = []

    def load(source, target):
        copy = pltpu.make_async_copy(source, target, load_sem.at[len(loads)])
        copy.start()
        loads.append(copy)

    def part(source, which):
        return source.at[:, :, lanes(which)] if len(source.shape) == 3 else source.at[:, lanes(which)]

    for source, target in edge_data:
        load(part(source, side), target.at[0])
    load(plain_hbm, plain_ref)
    load(rhs_ref.at[:, lanes(side)], rhs_all.at[rows(h)])
    load(unit_hbm, unit_ref)
    load(swap_hbm, swap_ref)
    load(unit_t_hbm, unit_t_ref)
    for source, target in edge_data:
        load(part(source, 1 - side), target.at[1])

    barrier = pltpu.get_barrier_semaphore()

    def greet(offset, carry):
        pl.semaphore_signal(barrier, inc=1, device_id=device_at(lax.rem(place + offset, places)), device_id_type=MESH)
        return carry

    lax.fori_loop(1, places, greet, 0)
    extra = [o for o in range(1, n_harm) if o % group != 0]
    for o in extra:
        pl.semaphore_signal(barrier, inc=1, device_id=(lax.rem(h + o, n_harm), s), device_id_type=MESH)
    pl.semaphore_wait(barrier, places - 1 + len(extra))

    rhs_copies = []
    for o in range(1, n_harm):
        peer = lax.rem(h + o, n_harm)
        copy = pltpu.make_async_remote_copy(
            src_ref=rhs_ref.at[:, lanes(side_of(peer, s))],
            dst_ref=rhs_all.at[rows(h)],
            send_sem=rhs_send.at[o - 1],
            recv_sem=rhs_recv.at[o - 1],
            device_id=(peer, s),
            device_id_type=MESH,
        )
        copy.start()
        rhs_copies.append(copy)
    cross = device_at(lax.rem(place + places + 2 * side - 1, places))
    cross_copies = []
    for i, (source, target) in enumerate(edge_data):
        copy = pltpu.make_async_remote_copy(
            src_ref=part(source, side),
            dst_ref=target.at[2],
            send_sem=cross_send.at[i],
            recv_sem=cross_recv.at[i],
            device_id=cross,
            device_id_type=MESH,
        )
        copy.start()
        cross_copies.append(copy)

    lane_index = lax.broadcasted_iota(jnp.int32, (1, 128), 1)
    near = lax.broadcasted_iota(jnp.int32, (harmonics, own), 1) < IF
    left = device_at(lax.rem(place + places - 1, places))
    right = device_at(lax.rem(place + 1, places))
    halo_copies = []

    def send_halo(k, source):
        for way, target in ((0, right), (1, left)):
            copy = pltpu.make_async_remote_copy(
                src_ref=source,
                dst_ref=halo.at[k, way],
                send_sem=halo_send.at[k, way],
                recv_sem=halo_recv.at[k, way],
                device_id=target,
                device_id_type=MESH,
            )
            copy.start()
            halo_copies.append(copy)

    def total_of(product):
        return jnp.sum(jnp.sum(product, axis=0, keepdims=True), axis=1, keepdims=True)

    def send_dots(k, products):
        row = jnp.zeros((1, 128), jnp.float32)
        for i, product in enumerate(products):
            row = jnp.where(lane_index == i, total_of(product), row)
        msg[k] = row

        def send(offset, carry):
            pltpu.make_async_remote_copy(
                src_ref=msg.at[k],
                dst_ref=dots_in.at[k, offset - 1],
                send_sem=dot_send.at[k],
                recv_sem=dot_recv.at[k],
                device_id=device_at(lax.rem(place + offset, places)),
                device_id_type=MESH,
            ).start()
            return carry

        lax.fori_loop(1, places, send, 0)

    def wait_dots(sem, k):
        pltpu.make_async_copy(dots_in.at[k], dots_in.at[k], sem.at[k]).wait()

    def receive_dots(k, count):
        wait_dots(dot_recv, k)
        row = msg[k] + jnp.sum(dots_in[k], axis=0)
        return [row[:, i : i + 1] for i in range(count)]

    for copy in loads:
        copy.wait()
    start = place * own
    total_nodes = own * places
    diagonal = mass_ref[0]
    here = start + lax.broadcasted_iota(jnp.int32, (1, own), 1)
    for d in range(degree):
        used = nbr_ref[0, d : d + 1, :] != here
        diagonal = diagonal + jnp.where(used, mean_ref[0, d : d + 1, :], 0.0)
    last = ITERS // 2
    send_dots(last, [diagonal])

    first_row = lax.broadcasted_iota(jnp.int32, (half, own), 0) == 0

    def prepare(where_to, ripple, mean, spot, hot):
        height = hot.shape[0]
        row_index = lax.broadcasted_iota(jnp.int32, (height, own), 0)
        for d in range(degree):
            spectrum = dot_high(plain_ref[...], ripple(d))
            real, imag = spectrum[:half], spectrum[half:]
            k_re[where_to, d] = real + mean(d)
            k_re2[where_to, d] = jnp.where(first_row, imag, real) + mean(d)
            k_im[where_to, d] = jnp.where(first_row, 0.0, imag)
            hot[:, d * own : (d + 1) * own] = jnp.where(row_index == spot(d), 1.0, 0.0).astype(jnp.bfloat16)

    for copy in rhs_copies:
        copy.wait_recv()
    field[0] = dot_high(unit_ref[...], rhs_all[...])
    send_halo(0, field.at[0])
    prepare(
        0,
        lambda d: rip_ref[0, :, d, :],
        lambda d: mean_ref[0, d : d + 1, :],
        lambda d: jnp.bitwise_and(nbr_ref[0, d : d + 1, :] - start, own2 - 1),
        hot_own,
    )
    for copy in cross_copies:
        copy.wait_recv()
    lane_full = lax.broadcasted_iota(jnp.int32, (harmonics, own), 1)
    from_partner = jnp.where(lane_full < IF, 0, 1) == side

    def ghost(ref, index):
        partner, outer = ref[(1, *index)], ref[(2, *index)]
        return jnp.where(from_partner[: partner.shape[0]], partner, outer)

    def ghost_spot(d):
        place_of = ghost(nbr_ref, (slice(d, d + 1), slice(None))) - start
        place_of = jnp.where(place_of < 0, place_of + total_nodes, place_of)
        return jnp.where(place_of >= total_nodes - own, place_of - (total_nodes - 3 * own), place_of)

    prepare(
        1,
        lambda d: ghost(rip_ref, (slice(None), d, slice(None))),
        lambda d: ghost(mean_ref, (slice(d, d + 1), slice(None))),
        ghost_spot,
        hot_ghost,
    )
    whole_row = (slice(None), slice(None))
    wait_dots(dot_recv, last)
    theta = jnp.sum(msg[last] + jnp.sum(dots_in[last], axis=0), axis=1, keepdims=True) / total_nodes
    mass = [mass_ref[0] - theta, ghost(mass_ref, whole_row) - theta]
    eddy = [eddy_ref[0], ghost(eddy_ref, whole_row)]

    def stack(*tiles):
        pieces = [split_parts(tile, 3) for tile in tiles]
        return jnp.concatenate([jnp.concatenate(row, axis=1) for row in zip(*pieces)], axis=0)

    def operate(which, vector, stacked, hot):
        high, low = split_parts(vector, 2)
        swapped = jnp.dot(
            swap_ref[...], jnp.concatenate([high, high, low, low], axis=0),
            preferred_element_type=jnp.float32,
        )
        total = mass[which] * vector + eddy[which] * swapped
        v_re, v_im = vector[:half], vector[half:]
        sum_re, sum_im = total[:half], total[half:]
        for d in range(0, degree, 2):
            far = jnp.dot(stacked, hot[:, d * own : (d + 2) * own], preferred_element_type=jnp.float32)
            far = far[:harmonics] + far[harmonics : 2 * harmonics] + far[2 * harmonics :]
            for e in range(2):
                g_re = v_re - far[:half, e * own : (e + 1) * own]
                g_im = v_im - far[half:, e * own : (e + 1) * own]
                re, re2, im = k_re[which, d + e], k_re2[which, d + e], k_im[which, d + e]
                sum_re += re * g_re - im * g_im
                sum_im += re2 * g_im + im * g_re
        return jnp.concatenate([sum_re, sum_im], axis=0)

    def operate_twice(k, vector):
        halo_copies[2 * k].wait_recv()
        halo_copies[2 * k + 1].wait_recv()
        before, after = halo[k, 0], halo[k, 1]
        outer = jnp.where(near, after, before)
        once = operate(0, vector, stack(vector, outer), hot_own)
        once_outer = operate(1, outer, stack(vector, after, before), hot_ghost)
        return once, operate(0, once, stack(once, once_outer), hot_own)

    rhs = field[0]
    first, second = operate_twice(0, rhs)
    field[1] = second
    send_halo(1, field.at[1])
    send_dots(0, [rhs * rhs, rhs * first, rhs * second, first * first, first * second, second * second])
    third, fourth = operate_twice(1, second)
    rr, *found = receive_dots(0, 6)
    per_rr = 1.0 / rr
    beta = jnp.sqrt(rr)
    inverse = 1.0 / beta
    basis[0] = rhs * inverse
    image[0] = first * inverse
    image2[0] = second * inverse
    third, fourth = third * inverse, fourth * inverse
    found = [value * per_rr for value in found]
    fit = LeastSquares(beta)
    shifted = []
    pending = []

    def flush():
        for column in pending:
            i = len(fit.triangle)
            fit.add(column[:i] + [column[i] + theta] + column[i + 1 :])
        pending.clear()

    for m in range(0, ITERS, 2):
        on_more = m + 2 < ITERS
        x1, x2 = image[m], image2[m]
        if m > 0:
            if on_more:
                send_halo(m // 2 + 1, image2.at[m])
            kept = [basis[i] for i in range(m + 1)]
            send_dots(
                m // 2,
                [v * x1 for v in kept] + [v * x2 for v in kept] + [x1 * x1, x1 * x2, x2 * x2],
            )
            if on_more:
                third, fourth = operate_twice(m // 2 + 1, x2)
            flush()
            found = receive_dots(m // 2, 2 * m + 5)
        dot1, dot2 = found[: m + 1], found[m + 1 : 2 * m + 2]
        s11, s12, s22 = found[2 * m + 2 :]
        for p, q in zip(dot1, dot2):
            s11, s12, s22 = s11 - p * p, s12 - p * q, s22 - q * q
        length1 = jnp.sqrt(s11)
        scale1 = 1.0 / length1
        dot2.append(s12 * scale1)
        length2 = jnp.sqrt(s22 - dot2[-1] * dot2[-1])
        scale2 = 1.0 / length2
        column = dot1 + [length1]
        shifted.append(column)
        pending.append(column)
        column = dot2 + [length2]
        for i, value in enumerate(dot1):
            for k, entry in enumerate(shifted[i]):
                column[k] = column[k] - value * entry
        column = [entry * scale1 for entry in column]
        shifted.append(column)
        pending.append(column)
        new_v, new_p = x1, x2
        for i, value in enumerate(dot1):
            new_v = new_v - value * basis[i]
            new_p = new_p - value * image[i]
        basis[m + 1] = new_v * scale1
        image[m + 1] = new_p * scale1
        if on_more:
            new_q = third
            for i, value in enumerate(dot1):
                new_q = new_q - value * image2[i]
            image2[m + 1] = new_q * scale1
            new_v, new_p, new_q = x2, third, fourth
            for i, value in enumerate(dot2):
                new_v = new_v - value * basis[i]
                new_p = new_p - value * image[i]
                new_q = new_q - value * image2[i]
            basis[m + 2] = new_v * scale2
            image[m + 2] = new_p * scale2
            image2[m + 2] = new_q * scale2
    flush()
    coeffs = fit.solve()
    correction = coeffs[0] * basis[0]
    product = coeffs[0] * image[0]
    for j in range(1, ITERS):
        correction = correction + coeffs[j] * basis[j]
        product = product + coeffs[j] * image[j]
    residual = rhs - product - theta * correction
    phys[0] = dot_high(unit_t_ref[...], correction)
    phys[1] = dot_high(unit_t_ref[...], residual)

    other = lax.rem(h + group, n_harm)
    final = pltpu.make_async_remote_copy(
        src_ref=phys.at[:, rows(other)],
        dst_ref=phys_in,
        send_sem=out_send,
        recv_sem=out_recv,
        device_id=(other, s),
        device_id_type=MESH,
    )
    final.start()
    corr_ref[:, lanes(side)] = phys[0, rows(h)]
    res_ref[:, lanes(side)] = phys[1, rows(h)]
    for copy in rhs_copies + cross_copies + halo_copies:
        copy.wait_send()
    for k in range(ITERS // 2 + 1):
        wait_dots(dot_send, k)
    final.wait()
    corr_ref[:, lanes(1 - side)] = phys_in[0]
    res_ref[:, lanes(1 - side)] = phys_in[1]


def per_device(n_harm, n_space, rhs_field, neighbors, nu_mean, nu_ripple, mass_coeff, eddy_coeff):
    block, own2 = rhs_field.shape
    own = own2 // 2
    harmonics, degree = nu_ripple.shape[:2]
    plain, unit, unit_t, swap_parts = tables(harmonics)
    places = 2 * n_space
    f32 = jnp.float32
    vmem = pl.BlockSpec(memory_space=pltpu.VMEM)
    dma = pltpu.SemaphoreType.DMA
    return pl.pallas_call(
        functools.partial(gmres_kernel, n_harm, n_space),
        out_shape=(jax.ShapeDtypeStruct((block, own2), f32),) * 2,
        in_specs=[pl.BlockSpec(memory_space=pltpu.HBM)] * 10,
        out_specs=(vmem, vmem),
        scratch_shapes=[
            pltpu.VMEM((3, degree, own), neighbors.dtype),
            pltpu.VMEM((3, degree, own), f32),
            pltpu.VMEM((3, harmonics, degree, own), f32),
            pltpu.VMEM((3, 1, own), f32),
            pltpu.VMEM((3, 1, own), f32),
            pltpu.VMEM((harmonics, harmonics), f32),
            pltpu.VMEM((harmonics, harmonics), f32),
            pltpu.VMEM((harmonics, harmonics), f32),
            pltpu.VMEM(swap_parts.shape, jnp.bfloat16),
            dma((15,)),
            dma((5,)),
            dma((5,)),
            pltpu.VMEM((harmonics, own), f32),
            pltpu.VMEM((own2, degree * own), jnp.bfloat16),
            pltpu.VMEM((3 * own, degree * own), jnp.bfloat16),
            pltpu.VMEM((2, degree, harmonics // 2, own), f32),
            pltpu.VMEM((2, degree, harmonics // 2, own), f32),
            pltpu.VMEM((2, degree, harmonics // 2, own), f32),
            pltpu.VMEM((ITERS, harmonics, own), f32),
            pltpu.VMEM((ITERS, harmonics, own), f32),
            pltpu.VMEM((ITERS, harmonics, own), f32),
            pltpu.VMEM((2, harmonics, own), f32),
            pltpu.VMEM((ITERS // 2, 2, harmonics, own), f32),
            pltpu.VMEM((ITERS // 2 + 1, 1, 128), f32),
            pltpu.VMEM((ITERS // 2 + 1, places - 1, 1, 128), f32),
            pltpu.VMEM((2, harmonics, own), f32),
            pltpu.VMEM((2, block, own), f32),
            dma((n_harm - 1,)),
            dma((n_harm - 1,)),
            dma((ITERS // 2, 2)),
            dma((ITERS // 2, 2)),
            dma((ITERS // 2 + 1,)),
            dma((ITERS // 2 + 1,)),
            dma,
            dma,
        ],
        compiler_params=pltpu.CompilerParams(
            collective_id=0, has_side_effects=True, vmem_limit_bytes=60 * 1024 * 1024
        ),
    )(
        rhs_field, neighbors, nu_mean, nu_ripple,
        mass_coeff.reshape(1, own2), eddy_coeff.reshape(1, own2),
        jnp.asarray(plain), jnp.asarray(unit), jnp.asarray(unit_t), jnp.asarray(swap_parts),
    )


def solution(mesh):
    return jax.shard_map(
        functools.partial(per_device, mesh.shape["harm"], mesh.shape["space"]),
        mesh=mesh,
        in_specs=(
            P("harm", "space"),
            P(None, "space"),
            P(None, "space"),
            P(None, None, "space"),
            P("space"),
            P("space"),
        ),
        out_specs=(P("harm", "space"), P("harm", "space")),
        check_vma=False,
    )
```

time: 66.3 us -> 45.6 us (0.69)
  Pallas kernels: 56.9 us -> 42.7 us
  local copies, waits for them, and re-layouts: 8.13 us -> 2 us
    pallas_call x1, Pallas kernels: 56.9 us -> 42.7 us  [per_device(): pl.pallas_call(functools.partial(gmres_kernel, n_harm, n_space), out_shap...]
    unnamed x22 -> x4, local copies, waits for them, and re-layouts: 8.13 us -> 2 us
where the time goes in v2:
time: 45.6 us; the launch traced here: 45.4 us
  Pallas kernels  42.7 us (94%)
  local copies, waits for them, and re-layouts  2 us (4%)
  between operations  0.65 us (1%)
    pallas_call x1, Pallas kernels, per_device(): pl.pallas_call(functools.partial(gmres_kernel, n_harm, n_space), out_shap...  42.7 us
    unnamed x4, local copies, waits for them, and re-layouts  2 us

profile of v2, /device:TPU:0, one launch (start us, length us, event | category | flops | bytes accessed | tf_op | source)
XLA Modules:
  0.0 45.4 jit_solution(499109016506509460)
XLA Ops:
  0.6 42.7 %shard_map.113 = (f32[32,256]{1,0:T(8,128)}, f32[32,256]{1,0:T(8,128)}) custom-call(f32[32,256]{1,0:T(8,128)} %rhs_ref.1, s32[8,256]{1,0:T(8,128)} %nbr_hbm.1, f32[8,256]{1,0:T(8,128)} %mean_hbm.1, f32[64,8,256]{2,1,0:T(8,128)} %rip_hbm.1, f32[1,256]{1,0:T(1,128)} %bitcast.2, f32[1,256]{1,0:T(1,128)} %bitcast.3, f32[64,64]{1,0:T(8,128)} %constant.8.clone.plain_hbm, ...), custom_call_target="tpu_custom_call" | custom-call | tf_op jit(solution)/shard_map/pallas_call | solution.py:443
  43.4 0.0 copy-start
  43.4 1.4 %copy.14 = f32[32,256]{1,0:T(8,128)} copy(f32[32,256]{1,0:T(8,128)} %get-tuple-element.4) | data formatting | bytes 65536
  44.8 0.0 copy-done
  44.8 0.6 %copy.15 = f32[32,256]{1,0:T(8,128)} copy(f32[32,256]{1,0:T(8,128)S(1)} %copy-done) | data formatting | bytes 65536
Async XLA Ops:
  43.4 1.4 %copy-start = (f32[32,256]{1,0:T(8,128)S(1)}, f32[32,256]{1,0:T(8,128)}, u32[]{:S(2)}) copy-start(f32[32,256]{1,0:T(8,128)} %get-tuple-element.5) | copy-start | bytes 98308

commit v3 on v2

--- a/solution.py
+++ b/solution.py
@@ -83,7 +83,7 @@
     plain_hbm, unit_hbm, unit_t_hbm, swap_hbm,
     corr_ref, res_ref,
     nbr_ref, mean_ref, rip_ref, mass_ref, eddy_ref, plain_ref, unit_ref, unit_t_ref, swap_ref, load_sem,
-    cross_send, cross_recv,
+    packed, cross_send, cross_recv,
     rhs_all, hot_own, hot_ghost, k_re, k_re2, k_im, basis, image, image2, field, halo, msg, dots_in, phys, phys_in,
     rhs_send, rhs_recv, halo_send, halo_recv, dot_send, dot_recv, out_send, out_recv,
 ):
@@ -105,8 +105,12 @@
     place = 2 * s + side
 
     def device_at(position):
-        space = position // 2
-        return (lax.rem(lax.rem(position, 2) + space, 2) * group + lane_rank, space)
+        space = lax.shift_right_logical(position, 1)
+        return (jnp.bitwise_and(position + space, 1) * group + lane_rank, space)
+
+    def around(offset):
+        position = place + offset
+        return device_at(jnp.where(position >= places, position - places, position))
 
     def lanes(which):
         return pl.ds(pl.multiple_of(which * own, own), own)
@@ -140,13 +144,102 @@
     barrier = pltpu.get_barrier_semaphore()
 
     def greet(offset, carry):
-        pl.semaphore_signal(barrier, inc=1, device_id=device_at(lax.rem(place + offset, places)), device_id_type=MESH)
+        pl.semaphore_signal(barrier, inc=1, device_id=around(offset), device_id_type=MESH)
         return carry
 
     lax.fori_loop(1, places, greet, 0)
     extra = [o for o in range(1, n_harm) if o % group != 0]
     for o in extra:
         pl.semaphore_signal(barrier, inc=1, device_id=(lax.rem(h + o, n_harm), s), device_id_type=MESH)
+
+    lane_index = lax.broadcasted_iota(jnp.int32, (1, 128), 1)
+    near = lax.broadcasted_iota(jnp.int32, (harmonics, own), 1) < IF
+    left = device_at(lax.rem(place + places - 1, places))
+    right = device_at(lax.rem(place + 1, places))
+    halo_copies = []
+
+    def send_halo(k, source):
+        for way, target in ((0, right), (1, left)):
+            copy = pltpu.make_async_remote_copy(
+                src_ref=source,
+                dst_ref=halo.at[k, way],
+                send_sem=halo_send.at[k, way],
+                recv_sem=halo_recv.at[k, way],
+                device_id=target,
+                device_id_type=MESH,
+            )
+            copy.start()
+            halo_copies.append(copy)
+
+    def total_of(product):
+        return jnp.sum(jnp.sum(product, axis=0, keepdims=True), axis=1, keepdims=True)
+
+    def send_dots(k, products):
+        row = jnp.zeros((1, 128), jnp.float32)
+        for i, product in enumerate(products):
+            row = jnp.where(lane_index == i, total_of(product), row)
+        msg[k] = row
+
+        def send(offset, carry):
+            pltpu.make_async_remote_copy(
+                src_ref=msg.at[k],
+                dst_ref=dots_in.at[k, offset - 1],
+                send_sem=dot_send.at[k],
+                recv_sem=dot_recv.at[k],
+                device_id=around(offset),
+                device_id_type=MESH,
+            ).start()
+            return carry
+
+        lax.fori_loop(1, places, send, 0)
+
+    def wait_dots(sem, k):
+        pltpu.make_async_copy(dots_in.at[k], dots_in.at[k], sem.at[k]).wait()
+
+    def receive_dots(k, count):
+        wait_dots(dot_recv, k)
+        row = msg[k] + jnp.sum(dots_in[k], axis=0)
+        return [row[:, i : i + 1] for i in range(count)]
+
+    for copy in loads:
+        copy.wait()
+    start = place * own
+    total_nodes = own * places
+    diagonal = mass_ref[0]
+    here = start + lax.broadcasted_iota(jnp.int32, (1, own), 1)
+    for d in range(degree):
+        used = nbr_ref[0, d : d + 1, :] != here
+        diagonal = diagonal + jnp.where(used, mean_ref[0, d : d + 1, :], 0.0)
+    last = ITERS // 2
+
+    first_row = lax.broadcasted_iota(jnp.int32, (half, own), 0) == 0
+
+    def prepare(where_to, ripple, mean, spot, hot):
+        height = hot.shape[0]
+        row_index = lax.broadcasted_iota(jnp.int32, (height, own), 0)
+        for d in range(degree):
+            spectrum = dot_high(plain_ref[...], ripple(d))
+            real, imag = spectrum[:half], spectrum[half:]
+            k_re[where_to, d] = real + mean(d)
+            k_re2[where_to, d] = jnp.where(first_row, imag, real) + mean(d)
+            k_im[where_to, d] = jnp.where(first_row, 0.0, imag)
+            hot[:, d * own : (d + 1) * own] = jnp.where(row_index == spot(d), 1.0, 0.0).astype(jnp.bfloat16)
+
+    prepare(
+        0,
+        lambda d: rip_ref[0, :, d, :],
+        lambda d: mean_ref[0, d : d + 1, :],
+        lambda d: jnp.bitwise_and(nbr_ref[0, d : d + 1, :] - start, own2 - 1),
+        hot_own,
+    )
+    outward = jnp.where(lax.broadcasted_iota(jnp.int32, (half, own), 1) < IF, 0, 1) == side
+    for d in range(degree):
+        folded = pltpu.roll(rip_ref[0, half:, d, :], IF, 1)
+        packed[0, :, d, :] = jnp.where(outward, rip_ref[0, :half, d, :], folded)
+    outgoing = [(source.at[0], target.at[2]) for source, target in (
+        (nbr_ref, nbr_ref), (mean_ref, mean_ref), (mass_ref, mass_ref), (eddy_ref, eddy_ref)
+    )] + [(packed.at[0], packed.at[1])]
+
     pl.semaphore_wait(barrier, places - 1 + len(extra))
 
     rhs_copies = []
@@ -164,10 +257,10 @@
         rhs_copies.append(copy)
     cross = device_at(lax.rem(place + places + 2 * side - 1, places))
     cross_copies = []
-    for i, (source, target) in enumerate(edge_data):
+    for i, (source, target) in enumerate(outgoing):
         copy = pltpu.make_async_remote_copy(
-            src_ref=part(source, side),
-            dst_ref=target.at[2],
+            src_ref=source,
+            dst_ref=target,
             send_sem=cross_send.at[i],
             recv_sem=cross_recv.at[i],
             device_id=cross,
@@ -176,91 +269,11 @@
         copy.start()
         cross_copies.append(copy)
 
-    lane_index = lax.broadcasted_iota(jnp.int32, (1, 128), 1)
-    near = lax.broadcasted_iota(jnp.int32, (harmonics, own), 1) < IF
-    left = device_at(lax.rem(place + places - 1, places))
-    right = device_at(lax.rem(place + 1, places))
-    halo_copies = []
-
-    def send_halo(k, source):
-        for way, target in ((0, right), (1, left)):
-            copy = pltpu.make_async_remote_copy(
-                src_ref=source,
-                dst_ref=halo.at[k, way],
-                send_sem=halo_send.at[k, way],
-                recv_sem=halo_recv.at[k, way],
-                device_id=target,
-                device_id_type=MESH,
-            )
-            copy.start()
-            halo_copies.append(copy)
-
-    def total_of(product):
-        return jnp.sum(jnp.sum(product, axis=0, keepdims=True), axis=1, keepdims=True)
-
-    def send_dots(k, products):
-        row = jnp.zeros((1, 128), jnp.float32)
-        for i, product in enumerate(products):
-            row = jnp.where(lane_index == i, total_of(product), row)
-        msg[k] = row
-
-        def send(offset, carry):
-            pltpu.make_async_remote_copy(
-                src_ref=msg.at[k],
-                dst_ref=dots_in.at[k, offset - 1],
-                send_sem=dot_send.at[k],
-                recv_sem=dot_recv.at[k],
-                device_id=device_at(lax.rem(place + offset, places)),
-                device_id_type=MESH,
-            ).start()
-            return carry
-
-        lax.fori_loop(1, places, send, 0)
-
-    def wait_dots(sem, k):
-        pltpu.make_async_copy(dots_in.at[k], dots_in.at[k], sem.at[k]).wait()
-
-    def receive_dots(k, count):
-        wait_dots(dot_recv, k)
-        row = msg[k] + jnp.sum(dots_in[k], axis=0)
-        return [row[:, i : i + 1] for i in range(count)]
-
-    for copy in loads:
-        copy.wait()
-    start = place * own
-    total_nodes = own * places
-    diagonal = mass_ref[0]
-    here = start + lax.broadcasted_iota(jnp.int32, (1, own), 1)
-    for d in range(degree):
-        used = nbr_ref[0, d : d + 1, :] != here
-        diagonal = diagonal + jnp.where(used, mean_ref[0, d : d + 1, :], 0.0)
-    last = ITERS // 2
-    send_dots(last, [diagonal])
-
-    first_row = lax.broadcasted_iota(jnp.int32, (half, own), 0) == 0
-
-    def prepare(where_to, ripple, mean, spot, hot):
-        height = hot.shape[0]
-        row_index = lax.broadcasted_iota(jnp.int32, (height, own), 0)
-        for d in range(degree):
-            spectrum = dot_high(plain_ref[...], ripple(d))
-            real, imag = spectrum[:half], spectrum[half:]
-            k_re[where_to, d] = real + mean(d)
-            k_re2[where_to, d] = jnp.where(first_row, imag, real) + mean(d)
-            k_im[where_to, d] = jnp.where(first_row, 0.0, imag)
-            hot[:, d * own : (d + 1) * own] = jnp.where(row_index == spot(d), 1.0, 0.0).astype(jnp.bfloat16)
-
     for copy in rhs_copies:
         copy.wait_recv()
     field[0] = dot_high(unit_ref[...], rhs_all[...])
     send_halo(0, field.at[0])
-    prepare(
-        0,
-        lambda d: rip_ref[0, :, d, :],
-        lambda d: mean_ref[0, d : d + 1, :],
-        lambda d: jnp.bitwise_and(nbr_ref[0, d : d + 1, :] - start, own2 - 1),
-        hot_own,
-    )
+    send_dots(last, [diagonal])
     for copy in cross_copies:
         copy.wait_recv()
     lane_full = lax.broadcasted_iota(jnp.int32, (harmonics, own), 1)
@@ -270,6 +283,11 @@
         partner, outer = ref[(1, *index)], ref[(2, *index)]
         return jnp.where(from_partner[: partner.shape[0]], partner, outer)
 
+    def ghost_ripple(d):
+        low = packed[1, :, d, :]
+        outer = jnp.concatenate([low, pltpu.roll(low, IF, 1)], axis=0)
+        return jnp.where(from_partner, rip_ref[1, :, d, :], outer)
+
     def ghost_spot(d):
         place_of = ghost(nbr_ref, (slice(d, d + 1), slice(None))) - start
         place_of = jnp.where(place_of < 0, place_of + total_nodes, place_of)
@@ -277,7 +295,7 @@
 
     prepare(
         1,
-        lambda d: ghost(rip_ref, (slice(None), d, slice(None))),
+        ghost_ripple,
         lambda d: ghost(mean_ref, (slice(d, d + 1), slice(None))),
         ghost_spot,
         hot_ghost,
@@ -448,7 +466,7 @@
         scratch_shapes=[
             pltpu.VMEM((3, degree, own), neighbors.dtype),
             pltpu.VMEM((3, degree, own), f32),
-            pltpu.VMEM((3, harmonics, degree, own), f32),
+            pltpu.VMEM((2, harmonics, degree, own), f32),
             pltpu.VMEM((3, 1, own), f32),
             pltpu.VMEM((3, 1, own), f32),
             pltpu.VMEM((harmonics, harmonics), f32),
@@ -456,6 +474,7 @@
             pltpu.VMEM((harmonics, harmonics), f32),
             pltpu.VMEM(swap_parts.shape, jnp.bfloat16),
             dma((15,)),
+            pltpu.VMEM((2, harmonics // 2, degree, own), f32),
             dma((5,)),
             dma((5,)),
             pltpu.VMEM((harmonics, own), f32),

time: 45.6 us -> 42.7 us (0.936)
  Pallas kernels: 42.7 us -> 39.9 us
    pallas_call x1, Pallas kernels: 42.7 us -> 39.9 us  [per_device(): pl.pallas_call(functools.partial(gmres_kernel, n_harm, n_space), out_shap...]
where the time goes in v3:
time: 42.7 us; the launch traced here: 42.5 us
  Pallas kernels  39.9 us (93%)
  local copies, waits for them, and re-layouts  2 us (5%)
  between operations  0.65 us (2%)
    pallas_call x1, Pallas kernels, per_device(): pl.pallas_call(functools.partial(gmres_kernel, n_harm, n_space), out_shap...  39.9 us
    unnamed x4, local copies, waits for them, and re-layouts  2 us

profile of v3, /device:TPU:0, one launch (start us, length us, event | category | flops | bytes accessed | tf_op | source)
XLA Modules:
  0.0 42.5 jit_solution(4572107097469797168)
XLA Ops:
  0.6 39.9 %shard_map.113 = (f32[32,256]{1,0:T(8,128)}, f32[32,256]{1,0:T(8,128)}) custom-call(f32[32,256]{1,0:T(8,128)} %rhs_ref.1, s32[8,256]{1,0:T(8,128)} %nbr_hbm.1, f32[8,256]{1,0:T(8,128)} %mean_hbm.1, f32[64,8,256]{2,1,0:T(8,128)} %rip_hbm.1, f32[1,256]{1,0:T(1,128)} %bitcast.2, f32[1,256]{1,0:T(1,128)} %bitcast.3, f32[64,64]{1,0:T(8,128)} %constant.8.clone.plain_hbm, ...), custom_call_target="tpu_custom_call" | custom-call | tf_op jit(solution)/shard_map/pallas_call | solution.py:461
  40.5 0.0 copy-start
  40.5 1.4 %copy.14 = f32[32,256]{1,0:T(8,128)} copy(f32[32,256]{1,0:T(8,128)} %get-tuple-element.4) | data formatting | bytes 65536
  41.9 0.0 copy-done
  41.9 0.6 %copy.15 = f32[32,256]{1,0:T(8,128)} copy(f32[32,256]{1,0:T(8,128)S(1)} %copy-done) | data formatting | bytes 65536
Async XLA Ops:
  40.5 1.4 %copy-start = (f32[32,256]{1,0:T(8,128)S(1)}, f32[32,256]{1,0:T(8,128)}, u32[]{:S(2)}) copy-start(f32[32,256]{1,0:T(8,128)} %get-tuple-element.5) | copy-start | bytes 98308

commit v4 on v3

--- a/solution.py
+++ b/solution.py
@@ -180,13 +180,14 @@
             row = jnp.where(lane_index == i, total_of(product), row)
         msg[k] = row
 
-        def send(offset, carry):
+        def send(step, carry):
+            offset = places - step
             pltpu.make_async_remote_copy(
                 src_ref=msg.at[k],
                 dst_ref=dots_in.at[k, offset - 1],
                 send_sem=dot_send.at[k],
                 recv_sem=dot_recv.at[k],
-                device_id=around(offset),
+                device_id=device_at(jnp.bitwise_xor(place, offset)),
                 device_id_type=MESH,
             ).start()
             return carry

time: 42.7 us -> 42.1 us (0.986)
  Pallas kernels: 39.9 us -> 39.3 us
    pallas_call x1, Pallas kernels: 39.9 us -> 39.3 us  [per_device(): pl.pallas_call(functools.partial(gmres_kernel, n_harm, n_space), out_shap...]
where the time goes in v4:
time: 42.1 us; the launch traced here: 41.9 us
  Pallas kernels  39.3 us (93%)
  local copies, waits for them, and re-layouts  2 us (5%)
  between operations  0.65 us (2%)
    pallas_call x1, Pallas kernels, per_device(): pl.pallas_call(functools.partial(gmres_kernel, n_harm, n_space), out_shap...  39.3 us
    unnamed x4, local copies, waits for them, and re-layouts  2 us

profile of v4, /device:TPU:0, one launch (start us, length us, event | category | flops | bytes accessed | tf_op | source)
XLA Modules:
  0.0 41.9 jit_solution(12864160854168707405)
XLA Ops:
  0.6 39.3 %shard_map.113 = (f32[32,256]{1,0:T(8,128)}, f32[32,256]{1,0:T(8,128)}) custom-call(f32[32,256]{1,0:T(8,128)} %rhs_ref.1, s32[8,256]{1,0:T(8,128)} %nbr_hbm.1, f32[8,256]{1,0:T(8,128)} %mean_hbm.1, f32[64,8,256]{2,1,0:T(8,128)} %rip_hbm.1, f32[1,256]{1,0:T(1,128)} %bitcast.2, f32[1,256]{1,0:T(1,128)} %bitcast.3, f32[64,64]{1,0:T(8,128)} %constant.8.clone.plain_hbm, ...), custom_call_target="tpu_custom_call" | custom-call | tf_op jit(solution)/shard_map/pallas_call | solution.py:462
  39.9 0.0 copy-start
  39.9 1.4 %copy.14 = f32[32,256]{1,0:T(8,128)} copy(f32[32,256]{1,0:T(8,128)} %get-tuple-element.4) | data formatting | bytes 65536
  41.3 0.0 copy-done
  41.3 0.6 %copy.15 = f32[32,256]{1,0:T(8,128)} copy(f32[32,256]{1,0:T(8,128)S(1)} %copy-done) | data formatting | bytes 65536
Async XLA Ops:
  39.9 1.4 %copy-start = (f32[32,256]{1,0:T(8,128)S(1)}, f32[32,256]{1,0:T(8,128)}, u32[]{:S(2)}) copy-start(f32[32,256]{1,0:T(8,128)} %get-tuple-element.5) | copy-start | bytes 98308
